TPU v7x, 256 devices: a whole 4x4x8 slice. The times are simulated.
256 devices in a mesh: acq: 16 (over z_lo, x), az: 16 (over z_hi, y, core).
Axes of the slice: x: 4, y: 4, z: 8 (z_hi: 2, z_lo: 4; z = z_hi * 4 + z_lo), core: 2. Of those that a mesh axis runs over, the one named last changes fastest.
Arguments:
- matched_images: bfloat16 [128, 2, 2048, 2048], P('acq', None, 'az'), may hold values from -6 to 6
- master_segment_duo: bfloat16 [2, 2, 2048, 2048], P(None, None, 'az', 'acq'), may hold values from -6 to 6
- along_track_whole_displacement: int32 [128, 128], P('acq', 'az'), may hold values from -1 to 0
- slant_whole_displacement: int32 [128, 128], P('acq', 'az'), may hold values from -1 to 0
- along_track_subpixel_filter: int32 [128, 128], P('acq', 'az'), may hold values from 0 to 15
- slant_subpixel_filter: int32 [128, 128], P('acq', 'az'), may hold values from 0 to 15
- tile_master_segment: int32 [128, 128], P('acq', 'az'), may hold values from 0 to 1
Outputs:
- coherence: float32 [128, 2, 512, 128], P('acq', None, 'az')
All inputs are finite; a program needn't handle non-finite values.
Results may differ from a plain program's by a relative error of at most 0.0003.
Values may be sent and summed in bfloat16 or wider, within the bound.
A program may use at most 320 MiB of HBM per device.

v0:
```python
import jax
import jax.numpy as jnp
from jax import lax
from jax.sharding import PartitionSpec as P

TAPS = 8
NFRAC = 16
TILE_HEIGHT = 16
HALO = 4


def padded_2(cells, sides, width):
    for axis, dim in sides:
        count = lax.axis_size(axis)
        ends = count - 1
        head = lax.slice_in_dim(cells, 0, width, axis=dim)
        tail = lax.slice_in_dim(cells, cells.shape[dim] - width, cells.shape[dim], axis=dim)
        cells = jnp.concatenate(
            [
                lax.ppermute(tail, axis, [(i, (i + 1) % count) for i in range(ends)]),
                cells,
                lax.ppermute(head, axis, [((i + 1) % count, i) for i in range(ends)]),
            ],
            axis=dim,
        )
    return cells


def kernel_table():
    fraction = jnp.arange(NFRAC, dtype=jnp.float32)[:, None] / NFRAC
    distance = jnp.arange(TAPS, dtype=jnp.float32)[None, :] - 3.0 - fraction
    kernel_taps = jnp.sinc(distance) * (0.5 + 0.5 * jnp.cos(jnp.pi * distance / 4.0))
    return kernel_taps / jnp.sum(kernel_taps, axis=1, keepdims=True)


def line_weights(shift, index, table):
    onehot = (index[:, :, None] == jnp.arange(NFRAC, dtype=jnp.int32)[None, None, :]).astype(
        jnp.float32
    )
    kernel_taps = jnp.sum(onehot[:, :, :, None] * table[None, None, :, :], axis=2)
    placed = (
        jnp.arange(TAPS + 1, dtype=jnp.int32)[None, None, None, :]
        == 1 + jnp.arange(TAPS, dtype=jnp.int32)[None, None, :, None] + shift[:, :, None, None]
    )
    weights = jnp.sum(kernel_taps[:, :, :, None] * placed.astype(jnp.float32), axis=2)
    return jnp.repeat(weights, TILE_HEIGHT, axis=1)


def resample(padded, az_weight, rg_weight):
    line_count = az_weight.shape[1]
    summed = az_weight[:, None, :, 0, None] * padded[:, :, 0:line_count, :]
    for tap in range(1, TAPS + 1):
        summed = summed + az_weight[:, None, :, tap, None] * padded[:, :, tap : tap + line_count, :]
    columns = summed.shape[3]
    widened = jnp.pad(summed, ((0, 0), (0, 0), (0, 0), (4, 4)))
    result = rg_weight[:, None, :, 0, None] * widened[:, :, :, 0:columns]
    for tap in range(1, TAPS + 1):
        result = result + rg_weight[:, None, :, tap, None] * widened[:, :, :, tap : tap + columns]
    return result


def looks(values):
    lead = values.shape[:-2]
    line_count = values.shape[-2]
    columns = values.shape[-1]
    shaped = values.reshape(lead + (line_count // 4, 4, columns // 16, 16))
    return jnp.sum(shaped, axis=(-3, -1))


def correlation_magnitude(coregistered, chosen_master_segment):
    real_s = coregistered[..., 0, :, :]
    imag_s = coregistered[..., 1, :, :]
    master_inphase = chosen_master_segment[..., 0, :, :]
    master_quadrature = chosen_master_segment[..., 1, :, :]
    cross_re = looks(real_s * master_inphase + imag_s * master_quadrature)
    cross_im = looks(imag_s * master_inphase - real_s * master_quadrature)
    power_sec = looks(real_s * real_s + imag_s * imag_s)
    power_ref = looks(master_inphase * master_inphase + master_quadrature * master_quadrature)
    inverse = 1.0 / jnp.sqrt(power_sec * power_ref + 1e-06)
    return jnp.stack([cross_re * inverse, cross_im * inverse], axis=-3)


def on_device(
    matched_images,
    master_segment_duo,
    along_track_whole_displacement,
    slant_whole_displacement,
    along_track_subpixel_filter,
    slant_subpixel_filter,
    tile_master_segment,
):
    table = kernel_table()
    secondaries = matched_images.shape[0]
    group_size = 2
    group_count = secondaries // group_size

    def regroup(values):
        return values.reshape((group_count, group_size) + values.shape[1:])

    extended = padded_2(matched_images, (("az", 2),), HALO)

    def shifted(group_items):
        (
            group_images,
            track_displaced,
            slant_displaced,
            track_filter_coefficients,
            slant_filter_coefficients,
        ) = group_items
        padded = group_images.astype(jnp.float32)
        return resample(
            padded,
            line_weights(track_displaced, track_filter_coefficients, table),
            line_weights(slant_displaced, slant_filter_coefficients, table),
        )

    segment_chooser = jnp.repeat(tile_master_segment, TILE_HEIGHT, axis=1)[:, None, :, None] == 1
    grouped_inputs = (
        regroup(extended),
        regroup(along_track_whole_displacement),
        regroup(slant_whole_displacement),
        regroup(along_track_subpixel_filter),
        regroup(slant_subpixel_filter),
    )
    gathered_track_entries = lax.all_gather(master_segment_duo, "acq", axis=3, tiled=True).astype(
        jnp.float32
    )

    def group_result(group_items):
        coregistered = shifted(group_items[:5])
        chosen_master_segment = jnp.where(
            group_items[5], gathered_track_entries[1][None], gathered_track_entries[0][None]
        )
        return correlation_magnitude(coregistered, chosen_master_segment)

    values = lax.map(group_result, grouped_inputs + (regroup(segment_chooser),))
    return values.reshape((secondaries,) + values.shape[2:])


def solution(mesh):
    return jax.shard_map(
        on_device,
        mesh=mesh,
        in_specs=(
            P("acq", None, "az", None),
            P(None, None, "az", "acq"),
            P("acq", "az"),
            P("acq", "az"),
            P("acq", "az"),
            P("acq", "az"),
            P("acq", "az"),
        ),
        out_specs=P("acq", None, "az", None),
        check_vma=False,
    )
```

profile of v0, /device:TPU:4, one launch (start us, length us, event | category | flops | bytes accessed | tf_op | source)
XLA Modules:
  0.0 506.8 jit_solution(17579977952032218586)
XLA Ops:
  15.3 8.7 %pad_maximum_fusion = bf16[8,2,136,2048]{3,2,1,0:T(8,128)(2,1)} fusion(bf16[8,2,4,2048]{3,2,1,0:T(4,128)(2,1)S(1)} %collective-permute-done.1, bf16[8,2,128,2048]{3,2,1,0:T(8,128)(2,1)} %param.9, bf16[8,2,4,2048]{3,2,1,0:T(4,128)(2,1)S(1)} %collective-permute-done), kind=kLoop, calls=%fused_computation.119 | loop fusion | flops 26738688 | bytes 17825792 | tf_op jit(solution)/shard_map/concatenate | solution.py:18
  24.0 64.4 %all-gather.2.cloned.1.call-done = bf16[2,2,128,2048]{3,2,1,0:T(8,128)(2,1)} async-done(((bf16[2,2,128,128]{3,2,1,0:T(8,128)(2,1)}), bf16[2,2,128,2048]{3,2,1,0:T(8,128)(2,1)}) %all-gather.2.cloned.1.call-update) | async-done | bytes 2097168 | tf_op jit(solution)/shard_map/all_gather | solution.py:125
  88.4 4.1 convert_element_type.43
  92.5 406.7 %while.13 = (s32[]{:T(128)}, f32[4,2,2,32,128]{4,3,2,1,0:T(8,128)S(1)}, s32[4,2,8]{2,1,0:T(2,128)}, s32[4,2,8]{2,1,0:T(2,128)}, s32[4,2,8]{2,1,0:T(2,128)}, /*in...) while((s32[]{:T(128)}, ...), condition=%wide.region_10.11_spmd.clone, body=%wide.region_1.10_spmd.clone.sunk | while | flops 46240104 | bytes 133099400 | solution.py:136
  97.0 5.8 %fusion.97 = f32[2,2,128,2048]{3,2,0,1:T(8,128)} fusion(f32[2,2,136,2048]{3,2,0,1:T(8,128)S(1)} %fusion.91, f32[2,128]{1,0:T(2,128)S(1)} %get-tuple-element.371, f32[2,128]{1,0:T(2,128)S(1)} %get-tuple-element.372, f32[2,128]{1,0:T(2,128)S(1)} %get-tuple-element.373, f32[2,128]{1,0:T(2,128)S(1)} %get-tuple-element.374, ...), kind=kLoop, calls=%fused_computation.2.clone.1 | loop fusion | flops 17825792 | bytes 41952256 | tf_op jit(solution)/shard_map/while/body/eval_jaxpr/add | solution.py:53
  103.2 18.1 %multiply_add_fusion.8 = f32[2,2,128,2048]{3,2,0,1:T(8,128)S(1)} fusion(f32[2,2,128,2048]{3,2,0,1:T(8,128)} %fusion.97, f32[2,128]{1,0:T(2,128)S(1)} %get-tuple-element.382, f32[2,128]{1,0:T(2,128)S(1)} %get-tuple-element.383, f32[2,128]{1,0:T(2,128)S(1)} %get-tuple-element.384, f32[2,128]{1,0:T(2,128)S(1)} %get-tuple-element.385, ...), kind=kLoop, calls=%fused_computation.18.clone.1 | loop fusion | flops 17825792 | bytes 8397824 | tf_op jit(solution)/shard_map/while/body/eval_jaxpr/add | solution.py:58
  122.6 3.4 multiply_add_fusion.9
  126.0 10.4 %add.764 = f32[2,32,4,128,16]{4,3,2,1,0:T(8,128)} reshape(f32[2,1,128,2048]{3,2,0,1:T(8,128)} %get-tuple-element.391) | data formatting | bytes 4194304 | tf_op jit(solution)/shard_map/while/body/eval_jaxpr/add | solution.py:75
  136.4 7.0 %reduce_sum.129 = f32[2,32,128]{2,1,0:T(8,128)S(1)} reduce(f32[2,32,4,128,16]{4,3,2,1,0:T(8,128)} %add.764, f32[]{:T(128)} %constant.82.clone.8..sunk), dimensions={2,4}, to_apply=%region_6.6 | reduce | flops 516096 | bytes 2129924 | tf_op jit(solution)/shard_map/while/body/eval_jaxpr/reduce_sum | solution.py:67
  143.3 10.4 %add.765 = f32[2,32,4,128,16]{4,3,2,1,0:T(8,128)} reshape(f32[2,1,128,2048]{3,2,0,1:T(8,128)} %get-tuple-element.392) | data formatting | bytes 4194304 | tf_op jit(solution)/shard_map/while/body/eval_jaxpr/add | solution.py:77
  153.8 7.0 %reduce_sum.130 = f32[2,32,128]{2,1,0:T(8,128)S(1)} reduce(f32[2,32,4,128,16]{4,3,2,1,0:T(8,128)} %add.765, f32[]{:T(128)} %constant.82.clone.8..sunk), dimensions={2,4}, to_apply=%region_7.7 | reduce | flops 516096 | bytes 2129924 | tf_op jit(solution)/shard_map/while/body/eval_jaxpr/reduce_sum | solution.py:67
  160.7 10.4 %add.766 = f32[2,32,4,128,16]{4,3,2,1,0:T(8,128)} reshape(f32[2,1,128,2048]{3,2,0,1:T(8,128)} %get-tuple-element.393) | data formatting | bytes 4194304 | tf_op jit(solution)/shard_map/while/body/eval_jaxpr/add | solution.py:78
  171.2 7.0 %reduce_sum.131 = f32[2,32,128]{2,1,0:T(8,128)S(1)} reduce(f32[2,32,4,128,16]{4,3,2,1,0:T(8,128)} %add.766, f32[]{:T(128)} %constant.82.clone.8..sunk), dimensions={2,4}, to_apply=%region_8.8 | reduce | flops 516096 | bytes 2129924 | tf_op jit(solution)/shard_map/while/body/eval_jaxpr/reduce_sum | solution.py:67
  178.1 9.0 %sub.455 = f32[2,32,4,128,16]{4,3,2,1,0:T(8,128)} reshape(f32[2,1,128,2048]{3,2,0,1:T(8,128)S(1)} %get-tuple-element.394) | data formatting | bytes 4194304 | tf_op jit(solution)/shard_map/while/body/eval_jaxpr/sub | solution.py:76
  187.1 7.0 %reduce_sum.132 = f32[2,32,128]{2,1,0:T(8,128)S(1)} reduce(f32[2,32,4,128,16]{4,3,2,1,0:T(8,128)} %sub.455, f32[]{:T(128)} %constant.82.clone.8..sunk), dimensions={2,4}, to_apply=%region_9.9 | reduce | flops 516096 | bytes 2129924 | tf_op jit(solution)/shard_map/while/body/eval_jaxpr/reduce_sum | solution.py:67
  198.7 5.8 %fusion.97 = f32[2,2,128,2048]{3,2,0,1:T(8,128)} fusion(f32[2,2,136,2048]{3,2,0,1:T(8,128)S(1)} %fusion.91, f32[2,128]{1,0:T(2,128)S(1)} %get-tuple-element.371, f32[2,128]{1,0:T(2,128)S(1)} %get-tuple-element.372, f32[2,128]{1,0:T(2,128)S(1)} %get-tuple-element.373, f32[2,128]{1,0:T(2,128)S(1)} %get-tuple-element.374, ...), kind=kLoop, calls=%fused_computation.2.clone.1 | loop fusion | flops 17825792 | bytes 41952256 | tf_op jit(solution)/shard_map/while/body/eval_jaxpr/add | solution.py:53
  204.9 18.1 %multiply_add_fusion.8 = f32[2,2,128,2048]{3,2,0,1:T(8,128)S(1)} fusion(f32[2,2,128,2048]{3,2,0,1:T(8,128)} %fusion.97, f32[2,128]{1,0:T(2,128)S(1)} %get-tuple-element.382, f32[2,128]{1,0:T(2,128)S(1)} %get-tuple-element.383, f32[2,128]{1,0:T(2,128)S(1)} %get-tuple-element.384, f32[2,128]{1,0:T(2,128)S(1)} %get-tuple-element.385, ...), kind=kLoop, calls=%fused_computation.18.clone.1 | loop fusion | flops 17825792 | bytes 8397824 | tf_op jit(solution)/shard_map/while/body/eval_jaxpr/add | solution.py:58
  224.3 3.4 multiply_add_fusion.9
  227.6 10.4 %add.764 = f32[2,32,4,128,16]{4,3,2,1,0:T(8,128)} reshape(f32[2,1,128,2048]{3,2,0,1:T(8,128)} %get-tuple-element.391) | data formatting | bytes 4194304 | tf_op jit(solution)/shard_map/while/body/eval_jaxpr/add | solution.py:75
  238.1 7.0 %reduce_sum.129 = f32[2,32,128]{2,1,0:T(8,128)S(1)} reduce(f32[2,32,4,128,16]{4,3,2,1,0:T(8,128)} %add.764, f32[]{:T(128)} %constant.82.clone.8..sunk), dimensions={2,4}, to_apply=%region_6.6 | reduce | flops 516096 | bytes 2129924 | tf_op jit(solution)/shard_map/while/body/eval_jaxpr/reduce_sum | solution.py:67
  245.0 10.4 %add.765 = f32[2,32,4,128,16]{4,3,2,1,0:T(8,128)} reshape(f32[2,1,128,2048]{3,2,0,1:T(8,128)} %get-tuple-element.392) | data formatting | bytes 4194304 | tf_op jit(solution)/shard_map/while/body/eval_jaxpr/add | solution.py:77
  255.4 7.0 %reduce_sum.130 = f32[2,32,128]{2,1,0:T(8,128)S(1)} reduce(f32[2,32,4,128,16]{4,3,2,1,0:T(8,128)} %add.765, f32[]{:T(128)} %constant.82.clone.8..sunk), dimensions={2,4}, to_apply=%region_7.7 | reduce | flops 516096 | bytes 2129924 | tf_op jit(solution)/shard_map/while/body/eval_jaxpr/reduce_sum | solution.py:67
  262.4 10.4 %add.766 = f32[2,32,4,128,16]{4,3,2,1,0:T(8,128)} reshape(f32[2,1,128,2048]{3,2,0,1:T(8,128)} %get-tuple-element.393) | data formatting | bytes 4194304 | tf_op jit(solution)/shard_map/while/body/eval_jaxpr/add | solution.py:78
  272.8 7.0 %reduce_sum.131 = f32[2,32,128]{2,1,0:T(8,128)S(1)} reduce(f32[2,32,4,128,16]{4,3,2,1,0:T(8,128)} %add.766, f32[]{:T(128)} %constant.82.clone.8..sunk), dimensions={2,4}, to_apply=%region_8.8 | reduce | flops 516096 | bytes 2129924 | tf_op jit(solution)/shard_map/while/body/eval_jaxpr/reduce_sum | solution.py:67
  279.8 9.0 %sub.455 = f32[2,32,4,128,16]{4,3,2,1,0:T(8,128)} reshape(f32[2,1,128,2048]{3,2,0,1:T(8,128)S(1)} %get-tuple-element.394) | data formatting | bytes 4194304 | tf_op jit(solution)/shard_map/while/body/eval_jaxpr/sub | solution.py:76
  288.8 7.0 %reduce_sum.132 = f32[2,32,128]{2,1,0:T(8,128)S(1)} reduce(f32[2,32,4,128,16]{4,3,2,1,0:T(8,128)} %sub.455, f32[]{:T(128)} %constant.82.clone.8..sunk), dimensions={2,4}, to_apply=%region_9.9 | reduce | flops 516096 | bytes 2129924 | tf_op jit(solution)/shard_map/while/body/eval_jaxpr/reduce_sum | solution.py:67
  300.3 5.8 %fusion.97 = f32[2,2,128,2048]{3,2,0,1:T(8,128)} fusion(f32[2,2,136,2048]{3,2,0,1:T(8,128)S(1)} %fusion.91, f32[2,128]{1,0:T(2,128)S(1)} %get-tuple-element.371, f32[2,128]{1,0:T(2,128)S(1)} %get-tuple-element.372, f32[2,128]{1,0:T(2,128)S(1)} %get-tuple-element.373, f32[2,128]{1,0:T(2,128)S(1)} %get-tuple-element.374, ...), kind=kLoop, calls=%fused_computation.2.clone.1 | loop fusion | flops 17825792 | bytes 41952256 | tf_op jit(solution)/shard_map/while/body/eval_jaxpr/add | solution.py:53
  306.6 18.1 %multiply_add_fusion.8 = f32[2,2,128,2048]{3,2,0,1:T(8,128)S(1)} fusion(f32[2,2,128,2048]{3,2,0,1:T(8,128)} %fusion.97, f32[2,128]{1,0:T(2,128)S(1)} %get-tuple-element.382, f32[2,128]{1,0:T(2,128)S(1)} %get-tuple-element.383, f32[2,128]{1,0:T(2,128)S(1)} %get-tuple-element.384, f32[2,128]{1,0:T(2,128)S(1)} %get-tuple-element.385, ...), kind=kLoop, calls=%fused_computation.18.clone.1 | loop fusion | flops 17825792 | bytes 8397824 | tf_op jit(solution)/shard_map/while/body/eval_jaxpr/add | solution.py:58
  326.0 3.4 multiply_add_fusion.9
  329.3 10.4 %add.764 = f32[2,32,4,128,16]{4,3,2,1,0:T(8,128)} reshape(f32[2,1,128,2048]{3,2,0,1:T(8,128)} %get-tuple-element.391) | data formatting | bytes 4194304 | tf_op jit(solution)/shard_map/while/body/eval_jaxpr/add | solution.py:75
  339.7 7.0 %reduce_sum.129 = f32[2,32,128]{2,1,0:T(8,128)S(1)} reduce(f32[2,32,4,128,16]{4,3,2,1,0:T(8,128)} %add.764, f32[]{:T(128)} %constant.82.clone.8..sunk), dimensions={2,4}, to_apply=%region_6.6 | reduce | flops 516096 | bytes 2129924 | tf_op jit(solution)/shard_map/while/body/eval_jaxpr/reduce_sum | solution.py:67
  346.7 10.4 %add.765 = f32[2,32,4,128,16]{4,3,2,1,0:T(8,128)} reshape(f32[2,1,128,2048]{3,2,0,1:T(8,128)} %get-tuple-element.392) | data formatting | bytes 4194304 | tf_op jit(solution)/shard_map/while/body/eval_jaxpr/add | solution.py:77
  357.1 7.0 %reduce_sum.130 = f32[2,32,128]{2,1,0:T(8,128)S(1)} reduce(f32[2,32,4,128,16]{4,3,2,1,0:T(8,128)} %add.765, f32[]{:T(128)} %constant.82.clone.8..sunk), dimensions={2,4}, to_apply=%region_7.7 | reduce | flops 516096 | bytes 2129924 | tf_op jit(solution)/shard_map/while/body/eval_jaxpr/reduce_sum | solution.py:67
  364.1 10.4 %add.766 = f32[2,32,4,128,16]{4,3,2,1,0:T(8,128)} reshape(f32[2,1,128,2048]{3,2,0,1:T(8,128)} %get-tuple-element.393) | data formatting | bytes 4194304 | tf_op jit(solution)/shard_map/while/body/eval_jaxpr/add | solution.py:78
  374.5 7.0 %reduce_sum.131 = f32[2,32,128]{2,1,0:T(8,128)S(1)} reduce(f32[2,32,4,128,16]{4,3,2,1,0:T(8,128)} %add.766, f32[]{:T(128)} %constant.82.clone.8..sunk), dimensions={2,4}, to_apply=%region_8.8 | reduce | flops 516096 | bytes 2129924 | tf_op jit(solution)/shard_map/while/body/eval_jaxpr/reduce_sum | solution.py:67
  381.5 9.0 %sub.455 = f32[2,32,4,128,16]{4,3,2,1,0:T(8,128)} reshape(f32[2,1,128,2048]{3,2,0,1:T(8,128)S(1)} %get-tuple-element.394) | data formatting | bytes 4194304 | tf_op jit(solution)/shard_map/while/body/eval_jaxpr/sub | solution.py:76
  390.5 7.0 %reduce_sum.132 = f32[2,32,128]{2,1,0:T(8,128)S(1)} reduce(f32[2,32,4,128,16]{4,3,2,1,0:T(8,128)} %sub.455, f32[]{:T(128)} %constant.82.clone.8..sunk), dimensions={2,4}, to_apply=%region_9.9 | reduce | flops 516096 | bytes 2129924 | tf_op jit(solution)/shard_map/while/body/eval_jaxpr/reduce_sum | solution.py:67
  402.0 5.8 %fusion.97 = f32[2,2,128,2048]{3,2,0,1:T(8,128)} fusion(f32[2,2,136,2048]{3,2,0,1:T(8,128)S(1)} %fusion.91, f32[2,128]{1,0:T(2,128)S(1)} %get-tuple-element.371, f32[2,128]{1,0:T(2,128)S(1)} %get-tuple-element.372, f32[2,128]{1,0:T(2,128)S(1)} %get-tuple-element.373, f32[2,128]{1,0:T(2,128)S(1)} %get-tuple-element.374, ...), kind=kLoop, calls=%fused_computation.2.clone.1 | loop fusion | flops 17825792 | bytes 41952256 | tf_op jit(solution)/shard_map/while/body/eval_jaxpr/add | solution.py:53
  408.3 18.1 %multiply_add_fusion.8 = f32[2,2,128,2048]{3,2,0,1:T(8,128)S(1)} fusion(f32[2,2,128,2048]{3,2,0,1:T(8,128)} %fusion.97, f32[2,128]{1,0:T(2,128)S(1)} %get-tuple-element.382, f32[2,128]{1,0:T(2,128)S(1)} %get-tuple-element.383, f32[2,128]{1,0:T(2,128)S(1)} %get-tuple-element.384, f32[2,128]{1,0:T(2,128)S(1)} %get-tuple-element.385, ...), kind=kLoop, calls=%fused_computation.18.clone.1 | loop fusion | flops 17825792 | bytes 8397824 | tf_op jit(solution)/shard_map/while/body/eval_jaxpr/add | solution.py:58
  427.6 3.4 multiply_add_fusion.9
  431.0 10.4 %add.764 = f32[2,32,4,128,16]{4,3,2,1,0:T(8,128)} reshape(f32[2,1,128,2048]{3,2,0,1:T(8,128)} %get-tuple-element.391) | data formatting | bytes 4194304 | tf_op jit(solution)/shard_map/while/body/eval_jaxpr/add | solution.py:75
  441.4 7.0 %reduce_sum.129 = f32[2,32,128]{2,1,0:T(8,128)S(1)} reduce(f32[2,32,4,128,16]{4,3,2,1,0:T(8,128)} %add.764, f32[]{:T(128)} %constant.82.clone.8..sunk), dimensions={2,4}, to_apply=%region_6.6 | reduce | flops 516096 | bytes 2129924 | tf_op jit(solution)/shard_map/while/body/eval_jaxpr/reduce_sum | solution.py:67
  448.4 10.4 %add.765 = f32[2,32,4,128,16]{4,3,2,1,0:T(8,128)} reshape(f32[2,1,128,2048]{3,2,0,1:T(8,128)} %get-tuple-element.392) | data formatting | bytes 4194304 | tf_op jit(solution)/shard_map/while/body/eval_jaxpr/add | solution.py:77
  458.8 7.0 %reduce_sum.130 = f32[2,32,128]{2,1,0:T(8,128)S(1)} reduce(f32[2,32,4,128,16]{4,3,2,1,0:T(8,128)} %add.765, f32[]{:T(128)} %constant.82.clone.8..sunk), dimensions={2,4}, to_apply=%region_7.7 | reduce | flops 516096 | bytes 2129924 | tf_op jit(solution)/shard_map/while/body/eval_jaxpr/reduce_sum | solution.py:67
  465.8 10.4 %add.766 = f32[2,32,4,128,16]{4,3,2,1,0:T(8,128)} reshape(f32[2,1,128,2048]{3,2,0,1:T(8,128)} %get-tuple-element.393) | data formatting | bytes 4194304 | tf_op jit(solution)/shard_map/while/body/eval_jaxpr/add | solution.py:78
  476.2 7.0 %reduce_sum.131 = f32[2,32,128]{2,1,0:T(8,128)S(1)} reduce(f32[2,32,4,128,16]{4,3,2,1,0:T(8,128)} %add.766, f32[]{:T(128)} %constant.82.clone.8..sunk), dimensions={2,4}, to_apply=%region_8.8 | reduce | flops 516096 | bytes 2129924 | tf_op jit(solution)/shard_map/while/body/eval_jaxpr/reduce_sum | solution.py:67
  483.2 9.0 %sub.455 = f32[2,32,4,128,16]{4,3,2,1,0:T(8,128)} reshape(f32[2,1,128,2048]{3,2,0,1:T(8,128)S(1)} %get-tuple-element.394) | data formatting | bytes 4194304 | tf_op jit(solution)/shard_map/while/body/eval_jaxpr/sub | solution.py:76
  492.2 7.0 %reduce_sum.132 = f32[2,32,128]{2,1,0:T(8,128)S(1)} reduce(f32[2,32,4,128,16]{4,3,2,1,0:T(8,128)} %sub.455, f32[]{:T(128)} %constant.82.clone.8..sunk), dimensions={2,4}, to_apply=%region_9.9 | reduce | flops 516096 | bytes 2129924 | tf_op jit(solution)/shard_map/while/body/eval_jaxpr/reduce_sum | solution.py:67
  (120 shorter events, 33.8 us)
Async XLA Ops:
  6.5 81.9 %all-gather.2.cloned.1.call-start = ((), (), s32[]{:S(2)}) async-start(), calls=%async_computation | async-start | bytes 2228224 | tf_op jit(solution)/shard_map/all_gather | solution.py:125
  8.8 4.1 collective-permute-start
  10.5 4.8 collective-permute-start.1
  103.2 18.1 %copy-start = (f32[2,2,128,2048]{3,2,1,0:T(8,128)S(1)}, f32[2,2,128,2048]{3,2,1,0:T(8,128)}, u32[]{:S(2)}) copy-start(f32[2,2,128,2048]{3,2,1,0:T(8,128)} %get-tuple-element.433) | copy-start | bytes 12582916 | tf_op jit(solution)/shard_map/while
  204.9 18.1 %copy-start = (f32[2,2,128,2048]{3,2,1,0:T(8,128)S(1)}, f32[2,2,128,2048]{3,2,1,0:T(8,128)}, u32[]{:S(2)}) copy-start(f32[2,2,128,2048]{3,2,1,0:T(8,128)} %get-tuple-element.433) | copy-start | bytes 12582916 | tf_op jit(solution)/shard_map/while
  306.6 18.1 %copy-start = (f32[2,2,128,2048]{3,2,1,0:T(8,128)S(1)}, f32[2,2,128,2048]{3,2,1,0:T(8,128)}, u32[]{:S(2)}) copy-start(f32[2,2,128,2048]{3,2,1,0:T(8,128)} %get-tuple-element.433) | copy-start | bytes 12582916 | tf_op jit(solution)/shard_map/while
  408.2 18.1 %copy-start = (f32[2,2,128,2048]{3,2,1,0:T(8,128)S(1)}, f32[2,2,128,2048]{3,2,1,0:T(8,128)}, u32[]{:S(2)}) copy-start(f32[2,2,128,2048]{3,2,1,0:T(8,128)} %get-tuple-element.433) | copy-start | bytes 12582916 | tf_op jit(solution)/shard_map/while
  499.2 0.7 copy-start.1
Sparse Core Ops, SparseCore 0:
  9.1 79.2 all-gather.1
where the time goes:
time: 509 us; the launch traced here: 507 us
  other arithmetic  249 us (49%)
  local copies, waits for them, and re-layouts  173 us (34%)
  waiting for transfers between devices  67.6 us (13%)
  between operations  13.4 us (3%)
    reduce_sum x16, other arithmetic, looks(): return jnp.sum(shaped, axis=(-3, -1))  112 us
    add x4, other arithmetic, resample(): result + rg_weight[:, None, :, tap, None] * widened[:, :, :, tap:tap + co...  72.4 us
    all_gather x1, waiting for transfers between devices, on_device(): lax.all_gather(master_segment_duo, 'acq', axis=3, tiled=True)  64.4 us
    add x4, local copies, waits for them, and re-layouts, correlation_magnitude(): power_sec = looks(real_s * real_s + imag_s * imag_s)  41.6 us
    add x4, local copies, waits for them, and re-layouts, correlation_magnitude(): master_inphase * master_inphase + master_quadrature * master_quadrature  41.6 us
    add x4, local copies, waits for them, and re-layouts, correlation_magnitude(): cross_re = looks(real_s * master_inphase + imag_s * master_quadrature)  41.6 us
    sub x4, local copies, waits for them, and re-layouts, correlation_magnitude(): cross_im = looks(imag_s * master_inphase - real_s * master_quadrature)  36.1 us
    add x4, other arithmetic, resample(): summed + az_weight[:, None, :, tap, None] * padded[:, :, tap:tap + line_c...  23.3 us
  transfers between devices with their start and end apart: 3, of which 2 were waited for; matrix products, arithmetic and copies ran while one was open for 2% of the time, Pallas kernels for 0%

commit v1 on v0

v1 whole, which is shorter than its diff:
```python
import jax
import jax.numpy as jnp
from jax import lax
from jax.experimental import pallas as pl
from jax.experimental.pallas import tpu as pltpu
from jax.sharding import PartitionSpec as P

TAPS = 8
NFRAC = 16
TILE_HEIGHT = 16
F32, BF16 = jnp.float32, jnp.bfloat16
MESH = pl.DeviceIdType.MESH


def kernel_table():
    fraction = jnp.arange(NFRAC, dtype=F32)[:, None] / NFRAC
    distance = jnp.arange(TAPS, dtype=F32)[None, :] - 3.0 - fraction
    kernel_taps = jnp.sinc(distance) * (0.5 + 0.5 * jnp.cos(jnp.pi * distance / 4.0))
    return kernel_taps / jnp.sum(kernel_taps, axis=1, keepdims=True)


def line_weights(shift, index, table):
    onehot = (index[:, :, None] == jnp.arange(NFRAC, dtype=jnp.int32)).astype(F32)
    taps = jnp.sum(onehot[:, :, :, None] * table[None, None], axis=2)
    placed = (
        jnp.arange(16, dtype=jnp.int32)[None, None, None, :]
        == 1 + jnp.arange(TAPS, dtype=jnp.int32)[None, None, :, None] + shift[:, :, None, None]
    )
    weights = jnp.sum(taps[:, :, :, None] * placed.astype(F32), axis=2)
    return jnp.repeat(jnp.swapaxes(weights, 1, 2), TILE_HEIGHT, axis=2)


def split(value):
    high = value.astype(BF16)
    return high, (value - high.astype(F32)).astype(BF16)


def kernel(
    x_hbm, m_ref, azw_ref, rgw_ref, sel_ref, out_ref,
    xs, edge, hsend, halo, mt, xt, ht, y, z, m32, sums, wmat,
    x_sem, e_sem, hs_sem, hr_sem, zs_sem, zr_sem, xs_sem, xr_sem,
):
    acq = lax.axis_index("acq")
    az = lax.axis_index("az")
    zc, xc = acq // 4, acq % 4
    right, left = zc * 4 + (xc + 1) % 4, zc * 4 + (xc + 3) % 4

    for part in range(2):
        rows = pl.ds(112 * (1 - part), 16)
        pltpu.make_async_copy(x_hbm.at[:, :, rows, :], edge.at[part], e_sem.at[part]).start()
    for s in range(8):
        pltpu.make_async_copy(x_hbm.at[s], xs.at[s], x_sem.at[s]).start()

    barrier = pltpu.get_barrier_semaphore()

    def greet(a, b):
        pl.semaphore_signal(barrier, inc=1, device_id=(a, b), device_id_type=MESH)

    greet(right, az)
    greet(left, az)
    pl.when(zc < 3)(lambda: greet(acq + 4, az))
    pl.when(zc > 0)(lambda: greet(acq - 4, az))
    pl.when(az < 15)(lambda: greet(acq, az + 1))
    pl.when(az > 0)(lambda: greet(acq, az - 1))
    for p in range(4):
        mt[acq, p] = m_ref[p // 2, p % 2].T
    many = 2 + jnp.where(zc < 3, 1, 0) + jnp.where(zc > 0, 1, 0)
    many = many + jnp.where(az < 15, 1, 0) + jnp.where(az > 0, 1, 0)
    pl.semaphore_wait(barrier, many)

    def z_copy(block, up):
        return pltpu.make_async_remote_copy(
            src_ref=mt.at[block * 4 + xc], dst_ref=mt.at[block * 4 + xc],
            send_sem=zs_sem.at[up, block], recv_sem=zr_sem.at[block],
            device_id=(acq + 4 if up else acq - 4, az), device_id_type=MESH,
        )

    def x_copy(block, way):
        origin = [xc, xc, (xc + 3) % 4, (xc + 1) % 4][way]
        part = [slice(0, 4), slice(0, 4), slice(0, 2), slice(2, 4)][way]
        ref = mt.at[block * 4 + origin, part]
        return pltpu.make_async_remote_copy(
            src_ref=ref, dst_ref=ref,
            send_sem=xs_sem.at[way, block], recv_sem=xr_sem.at[way, block],
            device_id=(right if way % 2 == 0 else left, az), device_id_type=MESH,
        )

    def h_copy(part):
        return pltpu.make_async_remote_copy(
            src_ref=hsend.at[part], dst_ref=halo.at[pl.ds(64 * part, 64), :],
            send_sem=hs_sem.at[part], recv_sem=hr_sem.at[part],
            device_id=(acq, az + 1 if part == 0 else az - 1), device_id_type=MESH,
        )

    def have(block):
        x_copy(block, 0).start()
        x_copy(block, 1).start()

    def relay(block):
        x_copy(block, 0).wait_recv()
        x_copy(block, 2).start()
        x_copy(block, 1).wait_recv()
        x_copy(block, 3).start()

    def last(block):
        x_copy(block, 2).wait_recv()
        x_copy(block, 3).wait_recv()

    pl.when(zc < 3)(lambda: z_copy(zc, 1).start())
    pl.when(zc > 0)(lambda: z_copy(zc, 0).start())
    have(zc)

    for part in range(2):
        rows = pl.ds(112 * (1 - part), 16)
        pltpu.make_async_copy(x_hbm.at[:, :, rows, :], edge.at[part], e_sem.at[part]).wait()
        for g in range(4):
            picks = []
            for i in range(4):
                sc = 4 * g + i
                tile = edge[part, sc // 2, sc % 2].astype(F32)
                picks.append(tile[12:16] if part == 0 else tile[0:4])
            hsend[part, 16 * g : 16 * g + 16, :] = jnp.concatenate(picks, axis=0).astype(BF16)

        @pl.when(az < 15 if part == 0 else az > 0)
        def _():
            h_copy(part).start()

        @pl.when(az == 0 if part == 0 else az == 15)
        def _():
            halo[64 * part : 64 * part + 64, :] = jnp.zeros((64, 2048), BF16)

    for s in range(8):
        pltpu.make_async_copy(x_hbm.at[s], xs.at[s], x_sem.at[s]).wait()

    @pl.loop(0, 16)
    def _(sc):
        for k in range(16):
            xt[sc, k * 128 : (k + 1) * 128, :] = xs[sc // 2, sc % 2, :, k * 128 : (k + 1) * 128].T

    pl.when(az > 0)(lambda: h_copy(0).wait_recv())
    pl.when(az < 15)(lambda: h_copy(1).wait_recv())

    @pl.loop(0, 16)
    def _(k):
        cols = pl.ds(pl.multiple_of(k * 128, 128), 128)
        ht[cols, :] = halo[:, cols].T

    def z_step(d):
        @pl.when(zc + d <= 3)
        def _():
            z_copy(zc + d, 0).wait_recv()
            pl.when(zc > 0)(lambda: z_copy(zc + d, 0).start())
            have(zc + d)

        @pl.when(zc - d >= 0)
        def _():
            z_copy(zc - d, 1).wait_recv()
            pl.when(zc < 3)(lambda: z_copy(zc - d, 1).start())
            have(zc - d)

    def each(d, step):
        pl.when(zc + d <= 3)(lambda: step(zc + d))
        pl.when(zc - d >= 0)(lambda: step(zc - d))

    zero8 = jnp.zeros((8, 128), F32)
    for c in range(2):
        y[c, 0:8, :] = zero8
        y[c, 2056:2064, :] = zero8
    rows = lax.broadcasted_iota(jnp.int32, (128, 128), 0)
    lanes = lax.broadcasted_iota(jnp.int32, (128, 128), 1)

    @pl.loop(0, 8)
    def _(s):
        @pl.when(s == 0)
        def _():
            relay(zc)
            z_step(1)

        @pl.when(s == 2)
        def _():
            each(1, relay)
            z_step(2)

        @pl.when(s == 4)
        def _():
            each(2, relay)
            z_step(3)

        @pl.when(s == 6)
        def _():
            each(3, relay)

        azw = [azw_ref[s, u : u + 1, :] for u in range(9)]
        own = jnp.zeros((128, 128), F32)
        for u in range(9):
            own = jnp.where(rows - lanes + 4 == u, azw[u], own)
        high, low = split(own)
        for c in range(2):
            base = 8 * s + 4 * c
            top = rows - base
            bottom = rows - 64 - base
            line = jnp.where(
                (top >= 0) & (top < 4),
                top - 4,
                jnp.where((bottom >= 0) & (bottom < 4), 128 + bottom, -100000),
            )
            ends = jnp.zeros((128, 128), F32)
            for u in range(9):
                ends = jnp.where(line - lanes + 4 == u, azw[u], ends)
            ends_high, ends_low = split(ends)
            wmat[c, 0:128, 0:128] = high
            wmat[c, 0:128, 128:256] = low
            wmat[c, 128:256, 0:128] = ends_high
            wmat[c, 128:256, 128:256] = ends_low
        for c in range(2):
            for k in range(8):
                block = slice(k * 256, (k + 1) * 256)
                lhs = jnp.concatenate([xt[2 * s + c, block, :], ht[block, :]], axis=1)
                res = jnp.dot(lhs, wmat[c], preferred_element_type=F32)
                y[c, 8 + k * 256 : 8 + (k + 1) * 256, :] = res[:, 0:128] + res[:, 128:256]
        w = [jnp.broadcast_to(rgw_ref[s, v : v + 1, :], (8, 128)) for v in range(9)]

        @pl.loop(0, 16)
        def _(j):
            base = pl.multiple_of(j * 128, 128)
            psum = None
            for c in range(2):
                win = [y[c, pl.ds(base + 4 + q, 8, stride=16), :] for q in range(8)]
                for k in range(16):
                    win.append(y[c, pl.ds(base + 12 + k, 8, stride=16), :])
                    acc = w[0] * win[k]
                    for v in range(1, 9):
                        acc = acc + w[v] * win[k + v]
                    z[s, j, c, k] = acc
                    sq = acc * acc
                    psum = sq if psum is None else psum + sq
            sums[s, 2, pl.ds(pl.multiple_of(j * 8, 8), 8), :] = psum

    last(zc)
    each(1, last)
    each(2, last)
    each(3, last)

    @pl.loop(0, 16)
    def _(j):
        for p in range(4):
            m32[p] = mt[j, p].astype(F32)
        rowsel = pl.ds(pl.multiple_of(j * 8, 8), 8)
        for m in range(2):
            ps = None
            for k in range(16):
                c = m32[2 * m, pl.ds(k, 8, stride=16), :]
                d = m32[2 * m + 1, pl.ds(k, 8, stride=16), :]
                t = c * c + d * d
                ps = t if ps is None else ps + t
            sums[8, m, rowsel, :] = ps

        @pl.loop(0, 8)
        def _(s):
            sel = jnp.broadcast_to(sel_ref[pl.ds(s, 1), :], (8, 128)) > 0.5
            re = im = None
            for k in range(16):
                at = pl.ds(k, 8, stride=16)
                a = z[s, j, 0, k]
                b = z[s, j, 1, k]
                c = jnp.where(sel, m32[2, at, :], m32[0, at, :])
                d = jnp.where(sel, m32[3, at, :], m32[1, at, :])
                t = a * c + b * d
                q = b * c - a * d
                re = t if re is None else re + t
                im = q if im is None else im + q
            sums[s, 0, rowsel, :] = re
            sums[s, 1, rowsel, :] = im

    e = (
        lax.broadcasted_iota(jnp.int32, (32, 128), 0)
        == lax.broadcasted_iota(jnp.int32, (32, 128), 1) // 4
    ).astype(BF16)

    def group(p):
        high, low = split(p)
        dn = (((1,), (1,)), ((), ()))
        return lax.dot_general(e, high, dn, preferred_element_type=F32) + lax.dot_general(
            e, low, dn, preferred_element_type=F32
        )

    @pl.loop(0, 8)
    def _(s):
        sel = sel_ref[pl.ds(s, 1), :] > 0.5
        pref = group(jnp.where(sel, sums[8, 1], sums[8, 0]))
        inverse = 1.0 / jnp.sqrt(group(sums[s, 2]) * pref + 1e-6)
        out_ref[s, 0] = group(sums[s, 0]) * inverse
        out_ref[s, 1] = group(sums[s, 1]) * inverse

    pl.when(az < 15)(lambda: h_copy(0).wait_send())
    pl.when(az > 0)(lambda: h_copy(1).wait_send())
    for block in range(4):
        pl.when((zc < 3) & (block <= zc))(lambda: z_copy(block, 1).wait_send())
        pl.when((zc > 0) & (block >= zc))(lambda: z_copy(block, 0).wait_send())
        for way in range(4):
            x_copy(block, way).wait_send()


def on_device(images, masters, az_shift, rg_shift, az_index, rg_index, segment):
    table = kernel_table()
    azw = line_weights(az_shift, az_index, table)
    rgw = line_weights(rg_shift, rg_index, table)
    sel = jnp.repeat(segment, TILE_HEIGHT, axis=1).astype(F32)
    vmem = pl.BlockSpec(memory_space=pltpu.VMEM)
    dma = pltpu.SemaphoreType.DMA
    return pl.pallas_call(
        kernel,
        out_shape=jax.ShapeDtypeStruct((8, 2, 32, 128), F32),
        in_specs=[pl.BlockSpec(memory_space=pl.ANY)] + [vmem] * 4,
        out_specs=vmem,
        scratch_shapes=[
            pltpu.VMEM((8, 2, 128, 2048), BF16),
            pltpu.VMEM((2, 8, 2, 16, 2048), BF16),
            pltpu.VMEM((2, 64, 2048), BF16),
            pltpu.VMEM((128, 2048), BF16),
            pltpu.VMEM((16, 4, 128, 128), BF16),
            pltpu.VMEM((16, 2048, 128), BF16),
            pltpu.VMEM((2048, 128), BF16),
            pltpu.VMEM((2, 2064, 128), F32),
            pltpu.VMEM((8, 16, 2, 16, 8, 128), F32),
            pltpu.VMEM((4, 128, 128), F32),
            pltpu.VMEM((9, 3, 128, 128), F32),
            pltpu.VMEM((2, 256, 256), BF16),
            dma((8,)),
            dma((2,)),
            dma((2,)),
            dma((2,)),
            dma((2, 4)),
            dma((4,)),
            dma((4, 4)),
            dma((4, 4)),
        ],
        compiler_params=pltpu.CompilerParams(
            collective_id=0, has_side_effects=True, vmem_limit_bytes=58 * 2**20
        ),
        name="resample",
    )(images, masters, azw, rgw, sel)


def solution(mesh):
    return jax.shard_map(
        on_device,
        mesh=mesh,
        in_specs=(
            P("acq", None, "az", None),
            P(None, None, "az", "acq"),
            P("acq", "az"),
            P("acq", "az"),
            P("acq", "az"),
            P("acq", "az"),
            P("acq", "az"),
        ),
        out_specs=P("acq", None, "az", None),
        check_vma=False,
    )
```

time: 509 us -> 68.7 us (0.13)
  the two profiles are of different devices: /device:TPU:4 before, /device:TPU:160 now
where the time goes in v1:
time: 68.7 us; the launch traced here: 68.4 us
  Pallas kernels  59.9 us (87%)
  local copies, waits for them, and re-layouts  4.6 us (7%)
  other arithmetic  3.81 us (6%)
    pallas_call x1, Pallas kernels, on_device(): pl.pallas_call(kernel, out_shape=jax.ShapeDtypeStruct((8, 2, 32, 128), F3...  59.9 us
    unnamed x1, local copies, waits for them, and re-layouts  1.67 us
    reshape x2, local copies, waits for them, and re-layouts, line_weights(): return jnp.repeat(jnp.swapaxes(weights, 1, 2), TILE_HEIGHT, axis=2)  1.62 us
    convert_element_type x2, other arithmetic, line_weights(): (index[:, :, None] == jnp.arange(NFRAC, dtype=jnp.int32)).astype(F32)  1.52 us

profile of v1, /device:TPU:160, one launch (start us, length us, event | category | flops | bytes accessed | tf_op | source)
XLA Modules:
  0.0 68.4 jit_solution(3607624210334250933)
XLA Ops:
  0.0 0.1 fusion.29
  0.1 0.1 broadcast_divide_fusion
  0.3 0.8 %fusion = f32[8,8,16]{2,1,0:T(8,128)S(1)} fusion(s32[8,8]{1,0:T(8,128)} %param.11), kind=kLoop, calls=%fused_computation.8 | loop fusion | flops 2048 | bytes 4352 | tf_op jit(solution)/shard_map/convert_element_type | solution.py:23
  1.0 0.8 %fusion.1 = f32[8,8,16]{2,1,0:T(8,128)S(1)} fusion(s32[8,8]{1,0:T(8,128)} %param.12), kind=kLoop, calls=%fused_computation.9 | loop fusion | flops 2048 | bytes 4352 | tf_op jit(solution)/shard_map/convert_element_type | solution.py:23
  1.8 0.2 multiply_reduce_fusion
  2.0 0.8 %broadcast_add_fusion = (s32[8,8,8]{2,1,0:T(8,128)S(1)}, s32[8,8,8]{2,1,0:T(8,128)S(1)}) fusion(s32[8,8]{1,0:T(8,128)} %param.10, s32[8]{0:T(128)S(1)} %iota_add_fusion.1, s32[8,8]{1,0:T(8,128)} %param.9), kind=kLoop, calls=%fused_computation.10 | loop fusion | flops 1024 | bytes 4640 | tf_op jit(solution)/shard_map/add | solution.py:27
  2.8 0.3 select_reduce_fusion
  3.2 0.1 copy.8
  3.2 0.2 broadcast_in_dim.11
  3.5 0.8 %reshape.124.azw_ref = f32[8,16,128]{2,1,0:T(8,128)} reshape(f32[8,16,8,16]{3,2,1,0:T(8,128)S(1)} %broadcast_in_dim.11) | data formatting | bytes 131072 | tf_op jit(solution)/shard_map/reshape | solution.py:30
  4.3 0.1 copy.9
  4.3 0.2 broadcast_in_dim.12
  4.6 0.8 %reshape.125.rgw_ref = f32[8,16,128]{2,1,0:T(8,128)} reshape(f32[8,16,8,16]{3,2,1,0:T(8,128)S(1)} %broadcast_in_dim.12) | data formatting | bytes 131072 | tf_op jit(solution)/shard_map/reshape | solution.py:30
  5.4 0.7 %convert_element_type.28 = f32[8,8]{1,0:T(8,128)S(1)} convert(s32[8,8]{1,0:T(8,128)} %param.13) | non-fusion elementwise | flops 64 | bytes 512 | tf_op jit(solution)/shard_map/convert_element_type | solution.py:308
  6.0 0.1 broadcast_in_dim.13
  6.1 0.7 convert_element_type.29.sel_ref
  6.8 59.9 %resample.1 = f32[8,2,32,128]{3,2,1,0:T(8,128)} custom-call(bf16[8,2,128,2048]{3,2,1,0:T(8,128)(2,1)} %x_hbm.1, bf16[2,2,128,128]{3,2,1,0:T(8,128)(2,1)} %m_ref.1, f32[8,16,128]{2,1,0:T(8,128)} %reshape.124.azw_ref, f32[8,16,128]{2,1,0:T(8,128)} %reshape.125.rgw_ref, f32[8,128]{1,0:T(8,128)} %convert_element_type.29.sel_ref), custom_call_target="tpu_custom_call" | custom-call | tf_op jit(solution)/shard_map/resample/pallas_call | solution.py:311
  66.7 1.7 %copy.11 = f32[8,2,32,128]{3,2,1,0:T(8,128)} copy(f32[8,2,32,128]{3,2,1,0:T(8,128)} %resample.1) | data formatting | bytes 524288
  (3 shorter events, 0.0 us)

commit v2 on v1

v2 whole, which is shorter than its diff:
```python
import numpy as np

import jax
import jax.numpy as jnp
from jax import lax
from jax.experimental import pallas as pl
from jax.experimental.pallas import tpu as pltpu
from jax.sharding import PartitionSpec as P

MESH = pl.DeviceIdType.MESH
F32, BF16 = jnp.float32, jnp.bfloat16
TAPS, NFRAC = 8, 16
R = 512
NB = R // 128
HEAD = 24


def filter_table():
    x = np.arange(TAPS)[None, :] - 3.0 - np.arange(NFRAC)[:, None] / NFRAC
    taps = np.sinc(x) * (0.5 + 0.5 * np.cos(np.pi * x / 4.0))
    return taps / taps.sum(axis=1, keepdims=True)


def split(value):
    high = value.astype(BF16)
    return high, (value - high.astype(F32)).astype(BF16)


def spread(ints):
    block = lax.broadcasted_iota(jnp.int32, (8, 128), 1) // 16
    out = jnp.zeros((8, 128), F32)
    for b in range(8):
        out = jnp.where(block == b, ints[:, b : b + 1].astype(F32), out)
    return out


def pick(index, column):
    out = jnp.full((8, 128), float(column[0]), F32)
    for f in range(1, NFRAC):
        out = jnp.where(index == float(f), float(column[f]), out)
    return out


def build_weights(i0, i1, i2, i3, i4, azw, rgw, flag):
    table = filter_table()
    az_back = spread(i0[...]) < -0.5
    az_index = spread(i2[...])
    rg_index = spread(i3[...])
    centre = pick(rg_index, table[:, 3])
    taps = [pick(az_index, table[:, t]) * centre for t in range(TAPS)]
    zero = jnp.zeros((8, 128), F32)
    for u in range(TAPS + 1):
        azw[u] = jnp.where(az_back, taps[u] if u < TAPS else zero, taps[u - 1] if u > 0 else zero)
    for t in range(TAPS):
        rgw[t] = pick(rg_index, table[:, t] / table[:, 3])
    flag[0] = spread(i1[...])
    flag[1] = spread(i4[...])


def build_matrices(azw, wmat):
    rows = lax.broadcasted_iota(jnp.int32, (128, 128), 0)
    lanes = lax.broadcasted_iota(jnp.int32, (128, 128), 1)
    trow = lax.broadcasted_iota(jnp.int32, (16, 128), 0)
    tlane = lax.broadcasted_iota(jnp.int32, (16, 128), 1)

    @pl.loop(0, 8)
    def _(s):
        weight = [azw[u, pl.ds(s, 1), :] for u in range(9)]

        def banded(offset):
            out = jnp.zeros(offset.shape, F32)
            for u in range(9):
                out = jnp.where(offset == u - 4, weight[u], out)
            return split(out)

        high, low = banded(rows - lanes)
        half = 8 * (s % 2)
        start = pl.multiple_of(16 * (s // 2), 16)
        for c in range(2):
            n = 2 * s + c
            wmat[n, 0:128, 0:128] = high
            wmat[n, 0:128, 128:256] = low
            wmat[n, 128:256, :] = jnp.zeros((128, 256), BF16)
            at = trow - half - 4 * c
            for side in range(2):
                line = jnp.where((at >= 0) & (at < 4), at + (-4, 128)[side], -1000)
                high_end, low_end = banded(line - tlane)
                block = pl.ds(128 + 64 * side + start, 16)
                wmat[n, block, 0:128] = high_end
                wmat[n, block, 128:256] = low_end


def azimuth(j, buf, xt, ht, wmat, s, c):
    n = 2 * s + c
    rows = pl.ds(pl.multiple_of(j * R, R), R)
    lhs = jnp.concatenate([xt[n, rows, :], ht[rows, :]], axis=1)
    res = jnp.dot(lhs, wmat[n], preferred_element_type=F32)
    buf[c, pl.ds(8 * HEAD + s, R, stride=8), :] = res[:, 0:128] + res[:, 128:256]


def carry(src, dst):
    for c in range(2):
        dst[c, 0 : 8 * HEAD, :] = src[c, 8 * R : 8 * (R + HEAD), :]


class Range:
    def __init__(self, j, buf, z, sums, rgw, flag):
        self.j, self.buf, self.z, self.sums = j, buf, z, sums
        self.w = [rgw[t] for t in range(TAPS)]
        self.back = flag[0] < -0.5
        self.raw = [None, None]
        self.win = [[], []]

    def need(self, c, q):
        row = self.buf[c, pl.ds(self.base + 8 * q, 8), :]
        before = self.raw[c] if self.raw[c] is not None else self.buf[c, pl.ds(self.base + 8 * q - 8, 8), :]
        self.raw[c] = row
        self.win[c] = (self.win[c] + [jnp.where(self.back, before, row)])[-8:]

    def box(self, i, first=8):
        psum = None
        w = self.w
        self.base = pl.multiple_of(i * 128, 128)
        for c in range(2):
            for k in range(16):
                q = first + k
                if not self.win[c]:
                    for d in range(-3, 4):
                        self.need(c, q + d)
                self.need(c, q + 4)
                win = self.win[c]
                acc = win[3]
                for t in (0, 1, 2, 4, 5, 6, 7):
                    acc = acc + w[t] * win[t]
                self.z[c, R * self.j + 16 * i + k] = acc
                sq = acc * acc
                psum = sq if psum is None else psum + sq
        self.sums[2, R // 16 * self.j + i] = psum


def resample(refs, hook):
    xt, ht, wmat, buf_a, buf_b, z, sums, rgw, flag = refs

    def half(j, cur, nxt):
        carry(cur, nxt)

        @pl.loop(0, 8)
        def _(i):
            hook(j, i)
            azimuth(j + 1, nxt, xt, ht, wmat, i, 0)
            azimuth(j + 1, nxt, xt, ht, wmat, i, 1)
            for b in range(NB):
                Range(j, cur, z, sums, rgw, flag).box(i * NB + b)

    for c in range(2):
        buf_a[c, 0 : 8 * HEAD, :] = jnp.zeros((8 * HEAD, 128), F32)

    @pl.loop(0, 8)
    def _(i):
        azimuth(0, buf_a, xt, ht, wmat, i, 0)
        azimuth(0, buf_a, xt, ht, wmat, i, 1)

    n = 2048 // R
    for p in range(n // 2 - 1):
        half(2 * p, buf_a, buf_b)
        half(2 * p + 1, buf_b, buf_a)
    half(n - 2, buf_a, buf_b)
    last = buf_b

    @pl.loop(0, 8 * NB)
    def _(i):
        Range(n - 1, last, z, sums, rgw, flag).box(i)

    for c in range(2):
        buf_a[c, 0 : 8 * HEAD, :] = last[c, 8 * R : 8 * (R + HEAD), :]
        buf_a[c, 8 * HEAD : 8 * (HEAD + 8), :] = jnp.zeros((64, 128), F32)
    Range(n, buf_a, z, sums, rgw, flag).box(0)


def cross_slab(j, mt, m32, mp, z, sums, flag):
    sel = flag[1] > 0.5

    def row(ref, r):
        return jnp.broadcast_to(ref[pl.ds(r, 1), :], (8, 128))

    for p in range(4):
        m32[p] = mt[j, p].astype(F32)
    for m in range(2):
        t = m32[2 * m] * m32[2 * m] + m32[2 * m + 1] * m32[2 * m + 1]
        mp[m] = jnp.sum(t.reshape(8, 16, 128), axis=1)

    @pl.loop(0, 8)
    def _(i):
        box = j * 8 + i
        sums[3, box + 1] = jnp.where(sel, row(mp.at[1], i), row(mp.at[0], i))
        re = im = None
        for k in range(16):
            r = 16 * i + k
            a = z[0, box * 16 + 16 + k]
            b = z[1, box * 16 + 16 + k]
            c = jnp.where(sel, row(m32.at[2], r), row(m32.at[0], r))
            d = jnp.where(sel, row(m32.at[3], r), row(m32.at[1], r))
            t = a * c + b * d
            q = b * c - a * d
            re = t if re is None else re + t
            im = q if im is None else im + q
        sums[0, box + 1] = re
        sums[1, box + 1] = im


def finish(sums, out_ref):
    e = (
        lax.broadcasted_iota(jnp.int32, (32, 128), 0)
        == lax.broadcasted_iota(jnp.int32, (32, 128), 1) // 4
    ).astype(BF16)
    dn = (((1,), (1,)), ((), ()))

    def group(q, s):
        flat = sums.at[q].reshape(129 * 8, 128)
        high, low = split(flat[pl.ds(8 + s, 128, stride=8), :])
        return lax.dot_general(e, high, dn, preferred_element_type=F32) + lax.dot_general(
            e, low, dn, preferred_element_type=F32
        )

    @pl.loop(0, 8)
    def _(s):
        g = [group(q, s) for q in range(4)]
        inverse = 1.0 / jnp.sqrt(g[2] * g[3] + 1e-6)
        out_ref[s, 0] = g[0] * inverse
        out_ref[s, 1] = g[1] * inverse

def kernel(
    x_hbm, m_ref, i0, i1, i2, i3, i4, out_ref,
    xs, edge, hsend, halo, mt, xt, ht, buf_a, buf_b, z, m32, mp, sums, azw, rgw, flag, wmat,
    x_sem, e_sem, hs_sem, hr_sem, zs_sem, zr_sem, xs_sem, xr_sem,
):
    acq = lax.axis_index("acq")
    az = lax.axis_index("az")
    zc, xc = acq // 4, acq % 4
    right, left = zc * 4 + (xc + 1) % 4, zc * 4 + (xc + 3) % 4
    inner = (zc == 1) | (zc == 2)
    low = zc < 2
    order = [
        zc,
        jnp.where(low, zc + 1, zc - 1),
        jnp.where(inner, jnp.where(low, 0, 3), jnp.where(low, 2, 1)),
        jnp.where(low, 3, 0),
    ]

    def edge_copy(part):
        rows = pl.ds(112 * (1 - part), 16)
        return pltpu.make_async_copy(x_hbm.at[:, :, rows, :], edge.at[part], e_sem.at[part])

    def x_load(s):
        return pltpu.make_async_copy(x_hbm.at[s], xs.at[s], x_sem.at[s])

    for part in range(2):
        edge_copy(part).start()
    for s in range(8):
        x_load(s).start()

    barrier = pltpu.get_barrier_semaphore()

    def greet(a, b):
        pl.semaphore_signal(barrier, inc=1, device_id=(a, b), device_id_type=MESH)

    greet(right, az)
    greet(left, az)
    for g in range(1, 4):
        greet(order[g] * 4 + xc, az)
    pl.when(az < 15)(lambda: greet(acq, az + 1))
    pl.when(az > 0)(lambda: greet(acq, az - 1))
    for p in range(4):
        mt[acq, p] = m_ref[p // 2, p % 2].T

    def z_copy(block):
        return pltpu.make_async_remote_copy(
            src_ref=mt.at[acq], dst_ref=mt.at[acq],
            send_sem=zs_sem.at[block], recv_sem=zr_sem.at[zc],
            device_id=(block * 4 + xc, az), device_id_type=MESH,
        )

    def z_wait(block):
        pltpu.make_async_remote_copy(
            src_ref=mt.at[acq], dst_ref=mt.at[block * 4 + xc],
            send_sem=zs_sem.at[block], recv_sem=zr_sem.at[block],
            device_id=(block * 4 + xc, az), device_id_type=MESH,
        ).wait_recv()

    def x_copy(block, way):
        origin = [xc, xc, (xc + 3) % 4, (xc + 1) % 4][way]
        part = [slice(0, 4), slice(0, 4), slice(0, 2), slice(2, 4)][way]
        ref = mt.at[block * 4 + origin, part]
        return pltpu.make_async_remote_copy(
            src_ref=ref, dst_ref=ref,
            send_sem=xs_sem.at[way, block], recv_sem=xr_sem.at[way, block],
            device_id=(right if way % 2 == 0 else left, az), device_id_type=MESH,
        )

    def h_copy(part):
        return pltpu.make_async_remote_copy(
            src_ref=hsend.at[part], dst_ref=halo.at[pl.ds(64 * part, 64), :],
            send_sem=hs_sem.at[part], recv_sem=hr_sem.at[part],
            device_id=(acq, az + 1 if part == 0 else az - 1), device_id_type=MESH,
        )

    def have(block):
        x_copy(block, 0).start()
        x_copy(block, 1).start()

    def relay(block):
        x_copy(block, 0).wait_recv()
        x_copy(block, 2).start()
        x_copy(block, 1).wait_recv()
        x_copy(block, 3).start()

    def last(block):
        x_copy(block, 2).wait_recv()
        x_copy(block, 3).wait_recv()

    for part in range(2):
        edge_copy(part).wait()
        for g in range(4):
            picks = []
            for i in range(4):
                sc = 4 * g + i
                tile = edge[part, sc // 2, sc % 2].astype(F32)
                picks.append(tile[12:16] if part == 0 else tile[0:4])
            hsend[part, 16 * g : 16 * g + 16, :] = jnp.concatenate(picks, axis=0).astype(BF16)

    many = 5 + jnp.where(az < 15, 1, 0) + jnp.where(az > 0, 1, 0)
    pl.semaphore_wait(barrier, many)
    for part in range(2):

        @pl.when(az < 15 if part == 0 else az > 0)
        def _():
            h_copy(part).start()

        @pl.when(az == 0 if part == 0 else az == 15)
        def _():
            halo[64 * part : 64 * part + 64, :] = jnp.zeros((64, 2048), BF16)

    for g in range(1, 4):
        z_copy(order[g]).start()
    have(zc)

    build_weights(i0, i1, i2, i3, i4, azw, rgw, flag)
    build_matrices(azw, wmat)

    @pl.loop(0, 8)
    def _(s):
        x_load(s).wait()

        @pl.loop(0, 2)
        def _(c):
            for k in range(16):
                xt[2 * s + c, k * 128 : (k + 1) * 128, :] = xs[s, c, :, k * 128 : (k + 1) * 128].T

    z_wait(order[1])
    have(order[1])
    relay(order[0])
    pl.when(az > 0)(lambda: h_copy(0).wait_recv())
    pl.when(az < 15)(lambda: h_copy(1).wait_recv())

    @pl.loop(0, 4)
    def _(k):
        for i in range(4):
            cols = pl.ds(pl.multiple_of(k * 512 + i * 128, 128), 128)
            ht[cols, :] = halo[:, cols].T

    def step_a():
        z_wait(order[2])
        have(order[2])

    def step_b():
        z_wait(order[3])
        have(order[3])

    steps = {
        0: ((0, step_a), (4, lambda: relay(order[1]))),
        1: ((0, step_b), (4, lambda: relay(order[2]))),
        2: ((4, lambda: relay(order[3])),),
    }

    def hook(j, i):
        for at, step in steps.get(j, ()):
            pl.when(i == at)(step)

    resample((xt, ht, wmat, buf_a, buf_b, z, sums, rgw, flag), hook)

    @pl.loop(0, 4)
    def _(g):
        block = jnp.where(
            g < 2, jnp.where(g == 0, order[0], order[1]), jnp.where(g == 2, order[2], order[3])
        )
        last(block)

        @pl.loop(0, 4)
        def _(x):
            cross_slab(block * 4 + x, mt, m32, mp, z, sums, flag)

    finish(sums, out_ref)

    pl.when(az < 15)(lambda: h_copy(0).wait_send())
    pl.when(az > 0)(lambda: h_copy(1).wait_send())
    for g in range(1, 4):
        z_copy(order[g]).wait_send()
    for block in range(4):
        for way in range(4):
            x_copy(block, way).wait_send()


def on_device(images, masters, az_shift, rg_shift, az_index, rg_index, segment):
    vmem = pl.BlockSpec(memory_space=pltpu.VMEM)
    dma = pltpu.SemaphoreType.DMA
    return pl.pallas_call(
        kernel,
        out_shape=jax.ShapeDtypeStruct((8, 2, 32, 128), F32),
        in_specs=[pl.BlockSpec(memory_space=pl.ANY)] + [vmem] * 6,
        out_specs=vmem,
        scratch_shapes=[
            pltpu.VMEM((8, 2, 128, 2048), BF16),
            pltpu.VMEM((2, 8, 2, 16, 2048), BF16),
            pltpu.VMEM((2, 64, 2048), BF16),
            pltpu.VMEM((128, 2048), BF16),
            pltpu.VMEM((16, 4, 128, 128), BF16),
            pltpu.VMEM((16, 2048, 128), BF16),
            pltpu.VMEM((2048, 128), BF16),
            pltpu.VMEM((2, 8 * (R + HEAD), 128), F32),
            pltpu.VMEM((2, 8 * (R + HEAD), 128), F32),
            pltpu.VMEM((2, 2064, 8, 128), F32),
            pltpu.VMEM((4, 128, 128), F32),
            pltpu.VMEM((2, 8, 128), F32),
            pltpu.VMEM((4, 129, 8, 128), F32),
            pltpu.VMEM((9, 8, 128), F32),
            pltpu.VMEM((8, 8, 128), F32),
            pltpu.VMEM((2, 8, 128), F32),
            pltpu.VMEM((16, 256, 256), BF16),
            dma((8,)),
            dma((2,)),
            dma((2,)),
            dma((2,)),
            dma((4,)),
            dma((4,)),
            dma((4, 4)),
            dma((4, 4)),
        ],
        compiler_params=pltpu.CompilerParams(
            collective_id=0, has_side_effects=True, vmem_limit_bytes=60 * 2**20
        ),
        name="resample",
    )(images, masters, az_shift, rg_shift, az_index, rg_index, segment)


def solution(mesh):
    return jax.shard_map(
        on_device,
        mesh=mesh,
        in_specs=(
            P("acq", None, "az", None),
            P(None, None, "az", "acq"),
            P("acq", "az"),
            P("acq", "az"),
            P("acq", "az"),
            P("acq", "az"),
            P("acq", "az"),
        ),
        out_specs=P("acq", None, "az", None),
        check_vma=False,
    )
```

time: 68.7 us -> 49.5 us (0.72)
  the two profiles are of different devices: /device:TPU:160 before, /device:TPU:25 now
where the time goes in v2:
time: 49.5 us; the launch traced here: 48.7 us
  Pallas kernels  47 us (95%)
  local copies, waits for them, and re-layouts  1.67 us (3%)
    pallas_call x1, Pallas kernels, on_device(): pl.pallas_call(kernel, out_shape=jax.ShapeDtypeStruct((8, 2, 32, 128), F3...  47 us
    unnamed x1, local copies, waits for them, and re-layouts  1.67 us

profile of v2, /device:TPU:25, one launch (start us, length us, event | category | flops | bytes accessed | tf_op | source)
XLA Modules:
  0.0 48.7 jit_solution(3365780492983645472)
XLA Ops:
  0.0 47.0 %resample.1 = f32[8,2,32,128]{3,2,1,0:T(8,128)} custom-call(bf16[8,2,128,2048]{3,2,1,0:T(8,128)(2,1)} %x_hbm.1, bf16[2,2,128,128]{3,2,1,0:T(8,128)(2,1)} %m_ref.1, s32[8,8]{1,0:T(8,128)} %i0.1, s32[8,8]{1,0:T(8,128)} %i1.1, s32[8,8]{1,0:T(8,128)} %i2.1, s32[8,8]{1,0:T(8,128)} %i3.1, s32[8,8]{1,0:T(8,128)} %i4.1), custom_call_target="tpu_custom_call" | custom-call | tf_op jit(solution)/shard_map/resample/pallas_call | solution.py:416
  47.1 1.7 %copy.9 = f32[8,2,32,128]{3,2,1,0:T(8,128)} copy(f32[8,2,32,128]{3,2,1,0:T(8,128)} %resample.1) | data formatting | bytes 524288

commit v3 on v2

v3 whole, which is shorter than its diff:
```python
import numpy as np

import jax
import jax.numpy as jnp
from jax import lax
from jax.experimental import pallas as pl
from jax.experimental.pallas import tpu as pltpu
from jax.sharding import PartitionSpec as P

MESH = pl.DeviceIdType.MESH
F32, BF16 = jnp.float32, jnp.bfloat16
TAPS, NFRAC = 8, 16
CHUNKS = 4
BOXES = 2


def filter_table():
    x = np.arange(TAPS)[None, :] - 3.0 - np.arange(NFRAC)[:, None] / NFRAC
    taps = np.sinc(x) * (0.5 + 0.5 * np.cos(np.pi * x / 4.0))
    return taps / taps.sum(axis=1, keepdims=True)


def split(value):
    high = value.astype(BF16)
    return high, (value - high.astype(F32)).astype(BF16)


def spread(ints):
    block = lax.broadcasted_iota(jnp.int32, (8, 128), 1) // 16
    out = jnp.zeros((8, 128), F32)
    for b in range(8):
        out = jnp.where(block == b, ints[:, b : b + 1].astype(F32), out)
    return out


def pick(index, column):
    out = jnp.full((8, 128), float(column[0]), F32)
    for f in range(1, NFRAC):
        out = jnp.where(index == float(f), float(column[f]), out)
    return out


def across(ints):
    lane = lax.broadcasted_iota(jnp.int32, (8, 128), 1)
    row = lax.broadcasted_iota(jnp.int32, (8, 128), 0)
    value = ints.astype(F32)
    both = jnp.where(lane % 8 < 4, value[:, 0:1], value[:, 7:8])
    mine = jnp.where(lane // 8 % 8 == row, both, 0.0)
    return jnp.broadcast_to(jnp.sum(mine, axis=0, keepdims=True), (8, 128))


def place(back, taps):
    zero = jnp.zeros((8, 128), F32)
    return [
        jnp.where(back, taps[u] if u < TAPS else zero, taps[u - 1] if u > 0 else zero)
        for u in range(TAPS + 1)
    ]


def build_weights(i0, i1, i2, i3, i4, azw, rgw, flag, eazw, ergw):
    table = filter_table()
    rg_index = spread(i3[...])
    az_index = spread(i2[...])
    centre = pick(rg_index, table[:, 3])
    taps = place(spread(i0[...]) < -0.5, [pick(az_index, table[:, t]) * centre for t in range(TAPS)])
    for u in range(TAPS + 1):
        azw[u] = taps[u]
    for t in range(TAPS):
        rgw[t] = pick(rg_index, table[:, t] / table[:, 3])
    flag[0] = spread(i1[...])
    flag[1] = spread(i4[...])
    flag[2] = across(i4[...])
    rg_index = across(i3[...])
    az_index = across(i2[...])
    taps = place(across(i0[...]) < -0.5, [pick(az_index, table[:, t]) for t in range(TAPS)])
    more = place(across(i1[...]) < -0.5, [pick(rg_index, table[:, t]) for t in range(TAPS)])
    for u in range(TAPS + 1):
        eazw[u] = taps[u]
        ergw[u] = more[u]


def azimuth_own(xs, xt_a, xt_b, y, azw, wait, steps):
    rows = lax.broadcasted_iota(jnp.int32, (128, 128), 0)
    lanes = lax.broadcasted_iota(jnp.int32, (128, 128), 1)
    for c in range(2):
        y[c, 0:64, :] = jnp.zeros((64, 128), F32)
        y[c, 8 * 2056 : 8 * 2064, :] = jnp.zeros((64, 128), F32)

    def turn(s, dst):
        for c in range(2):
            for k in range(16):
                part = slice(k * 128, (k + 1) * 128)
                dst[c, part, :] = xs[s, c, :, part].T

    def half(s, cur, nxt):
        pl.when(s < 7)(lambda: wait(s + 1))
        offset = rows - lanes
        own = jnp.zeros((128, 128), F32)
        for u in range(9):
            own = jnp.where(offset == u - 4, azw[u, pl.ds(s, 1), :], own)
        matrix = jnp.concatenate(split(own), axis=0)
        for c in range(2):
            for k in range(CHUNKS):
                n = 2048 // CHUNKS
                lhs = cur[c, k * n : (k + 1) * n, :]
                y[c, pl.ds(64 + 8 * n * k + s, n, stride=8), :] = jnp.dot(
                    jnp.concatenate([lhs, lhs], axis=1), matrix, preferred_element_type=F32
                )
        turn(jnp.minimum(s + 1, 7), nxt)

    wait(0)
    turn(0, xt_a)

    start = 0
    for stop, step in steps:

        @pl.loop(start, stop)
        def _(p):
            half(2 * p, xt_a, xt_b)
            half(2 * p + 1, xt_b, xt_a)

        step()
        start = stop


def range_filter(y, z, sums, rgw, flag, edge, et, steps):
    w = [rgw[t] for t in range(TAPS)]

    def boxes(i):
        back = flag[0] < -0.5
        base = pl.multiple_of(i * (128 * BOXES), 128)
        cols = pl.ds(pl.multiple_of(i % 16 * 128, 128), 128)
        block = edge[i // 32, pl.ds(i // 16 % 2 * 4, 4), :, :, cols].reshape(128, 128)
        et[i // 16, cols, :] = block.T
        psum = [None] * BOXES
        for c in range(2):

            def load(q):
                return y[c, pl.ds(base + 64 + 8 * q, 8), :]

            before, win = load(-4), []
            for q in range(-3, 16 * BOXES + 4):
                row = load(q)
                win = (win + [jnp.where(back, before, row)])[-8:]
                before = row
                k = q - 4
                if k < 0:
                    continue
                acc = win[3]
                for t in (0, 1, 2, 4, 5, 6, 7):
                    acc = acc + w[t] * win[t]
                z[c, 16 * BOXES * i + k] = acc
                sq = acc * acc
                b = k // 16
                psum[b] = sq if psum[b] is None else psum[b] + sq
        for b in range(BOXES):
            sums[2, BOXES * i + b] = psum[b]

    start = 0
    for stop, step in steps:
        pl.loop(start, stop)(boxes)
        step()
        start = stop


def edge_line(lane):
    return jnp.where(lane % 8 < 4, lane % 8, 120 + lane % 8)


def edge_matrices(eazw, ewm, gmat):
    row = lax.broadcasted_iota(jnp.int32, (128, 128), 0)
    lane = lax.broadcasted_iota(jnp.int32, (128, 128), 1)
    image = lane // 8 % 8 * 2 + lane // 64
    at = edge_line(lane)

    def banded(line, owner, where):
        offset = jnp.where(owner == image, line - at, 1000)
        out = jnp.zeros((128, 128), F32)
        for u in range(9):
            out = jnp.where(offset == u - 4, eazw[u, 0:1, :], out)
        high, low = split(out)
        ewm[where, 0:128] = high
        ewm[where, 128:256] = low

    for q in range(4):
        banded(row % 16 + (112 if q < 2 else 0), q % 2 * 8 + row // 16, slice(128 * q, 128 * q + 128))
    banded(jnp.where(row < 64, row % 4 - 4, 128 + row % 4), row % 64 // 4, slice(512, 640))
    hit = (row == at).astype(F32)
    left = lane < 64
    zero = jnp.zeros((128, 128), F32)
    gmat[0:128, 0:128] = jnp.where(left, hit, zero).astype(BF16)
    gmat[128:256, 0:128] = jnp.where(left, zero, hit).astype(BF16)
    gmat[0:128, 128:256] = jnp.where(left, zero, hit).astype(BF16)
    gmat[128:256, 128:256] = jnp.where(left, -hit, zero).astype(BF16)


def edge_filter(halo, et, ewm, ye, ze, ergw):
    @pl.loop(0, 4)
    def _(k):
        for i in range(4):
            cols = pl.ds(pl.multiple_of(k * 512 + i * 128, 128), 128)
            et[4, cols, :] = halo[:, cols].T

    for k in range(2):
        part = slice(1024 * k, 1024 * k + 1024)
        lhs = jnp.concatenate([et[q, part, :] for q in range(5)], axis=1)
        res = jnp.dot(lhs, ewm[...], preferred_element_type=F32)
        ye[8 + 1024 * k : 8 + 1024 * k + 1024, :] = res[:, 0:128] + res[:, 128:256]
    ye[0:8, :] = jnp.zeros((8, 128), F32)
    ye[2056:2064, :] = jnp.zeros((8, 128), F32)

    @pl.loop(0, 32)
    def _(k):
        base = pl.multiple_of(k * 64, 64)
        acc = ergw[0, 0:1, :] * ye[pl.ds(base + 4, 64), :]
        for u in range(1, 9):
            acc = acc + ergw[u, 0:1, :] * ye[pl.ds(base + 4 + u, 64), :]
        ze[pl.ds(base, 64), :] = acc


def edge_cross(j, mt, gmat, ze, esum, flag):
    sel = flag[2, 0:1, :] > 0.5
    m = [
        jnp.dot(
            jnp.concatenate([mt[j, 2 * q], mt[j, 2 * q + 1]], axis=1),
            gmat[...],
            preferred_element_type=F32,
        )
        for q in range(2)
    ]
    one = jnp.where(sel, m[1][:, 0:128], m[0][:, 0:128])
    two = jnp.where(sel, m[1][:, 128:256], m[0][:, 128:256])
    v = ze[pl.ds(pl.multiple_of(j * 128, 128), 128), :]
    for q, product in enumerate((v * one, v * two, v * v, one * one)):
        esum[q, pl.ds(pl.multiple_of(j * 8, 8), 8), :] = jnp.sum(product.reshape(8, 16, 128), axis=1)


def cross_slab(j, mt, m32, mp, z, sums, flag):
    sel = flag[1] > 0.5

    def row(ref, r):
        return jnp.broadcast_to(ref[pl.ds(r, 1), :], (8, 128))

    for q in range(2):
        rows = slice(128 * q, 128 * q + 128)
        for p in range(4):
            m32[p, rows] = mt[j + q, p].astype(F32)
        for m in range(2):
            t = m32[2 * m, rows] * m32[2 * m, rows] + m32[2 * m + 1, rows] * m32[2 * m + 1, rows]
            mp[m, 8 * q : 8 * q + 8] = jnp.sum(t.reshape(8, 16, 128), axis=1)

    @pl.loop(0, 8)
    def _(h):
        for i in (2 * h, 2 * h + 1):
            box = j * 8 + i
            sums[3, box] = jnp.where(sel, row(mp.at[1], i), row(mp.at[0], i))
            re = im = None
            for k in range(16):
                r = 16 * i + k
                a = z[0, box * 16 + k]
                b = z[1, box * 16 + k]
                c = jnp.where(sel, row(m32.at[2], r), row(m32.at[0], r))
                d = jnp.where(sel, row(m32.at[3], r), row(m32.at[1], r))
                t = a * c + b * d
                q = b * c - a * d
                re = t if re is None else re + t
                im = q if im is None else im + q
            sums[0, box] = re
            sums[1, box] = im


def finish(sums, esum, out_ref):
    dn = (((1,), (1,)), ((), ()))

    def folded(e, value):
        high, low = split(value)
        return lax.dot_general(e, high, dn, preferred_element_type=F32) + lax.dot_general(
            e, low, dn, preferred_element_type=F32
        )

    row = lax.broadcasted_iota(jnp.int32, (32, 128), 0)
    lane = lax.broadcasted_iota(jnp.int32, (32, 128), 1)
    lines = (row == lane // 4).astype(BF16)

    @pl.loop(0, 2)
    def _(p):
        for s in (4 * p, 4 * p + 1, 4 * p + 2, 4 * p + 3):
            g = [
                folded(lines, sums.at[q].reshape(1024, 128)[pl.ds(s, 128, stride=8), :])
                for q in range(4)
            ]
            inverse = 1.0 / jnp.sqrt(g[2] * g[3] + 1e-6)
            out_ref[s, 0] = g[0] * inverse
            out_ref[s, 1] = g[1] * inverse

    ends = ((row // 2 == lane // 8 % 8) & (row % 2 == lane % 8 // 4)).astype(BF16)
    g = [folded(ends, esum[q]) for q in range(4)]
    inverse = 1.0 / jnp.sqrt(g[2] * g[3] + 1e-6)
    for part in range(2):
        value = g[part] * inverse
        for s in range(8):
            out_ref[s, part, 0:1, :] = value[2 * s : 2 * s + 1, :]
            out_ref[s, part, 31:32, :] = value[2 * s + 1 : 2 * s + 2, :]

def kernel(
    x_hbm, m_ref, i0, i1, i2, i3, i4, out_ref,
    hsend, halo, mt,
    xs, edge, xt_a, xt_b, y, z, et, ye, ze, m32, mp, sums, esum, azw, rgw, flag, eazw, ergw, ewm, gmat,
    x_sem, e_sem, hs_sem, hr_sem, zs_sem, zr_sem, xs_sem, xr_sem,
):
    acq = lax.axis_index("acq")
    az = lax.axis_index("az")
    zc, xc = acq // 4, acq % 4
    right, left = zc * 4 + (xc + 1) % 4, zc * 4 + (xc + 3) % 4
    inner = (zc == 1) | (zc == 2)
    low = zc < 2
    order = [
        zc,
        jnp.where(low, zc + 1, zc - 1),
        jnp.where(inner, jnp.where(low, 0, 3), jnp.where(low, 2, 1)),
        jnp.where(low, 3, 0),
    ]

    def edge_copy(part):
        rows = pl.ds(112 * (1 - part), 16)
        return pltpu.make_async_copy(x_hbm.at[:, :, rows, :], edge.at[part], e_sem.at[part])

    def x_load(s):
        return pltpu.make_async_copy(x_hbm.at[s], xs.at[s], x_sem.at[s])

    for part in range(2):
        edge_copy(part).start()
    for s in range(8):
        x_load(s).start()

    barrier = pltpu.get_barrier_semaphore()

    def greet(a, b):
        pl.semaphore_signal(barrier, inc=1, device_id=(a, b), device_id_type=MESH)

    greet(right, az)
    greet(left, az)
    pl.when(zc < 3)(lambda: greet(acq + 4, az))
    pl.when(zc > 0)(lambda: greet(acq - 4, az))
    pl.when(az < 15)(lambda: greet(acq, az + 1))
    pl.when(az > 0)(lambda: greet(acq, az - 1))
    for p in range(4):
        mt[acq, p] = m_ref[p // 2, p % 2].T

    def z_copy(block, up):
        ref = mt.at[block * 4 + xc]
        return pltpu.make_async_remote_copy(
            src_ref=ref, dst_ref=ref,
            send_sem=zs_sem.at[up, block], recv_sem=zr_sem.at[block],
            device_id=(acq + 4 if up else acq - 4, az), device_id_type=MESH,
        )

    def x_copy(block, way):
        origin = [xc, xc, (xc + 3) % 4, (xc + 1) % 4][way]
        part = [slice(0, 4), slice(0, 4), slice(0, 2), slice(2, 4)][way]
        ref = mt.at[block * 4 + origin, part]
        return pltpu.make_async_remote_copy(
            src_ref=ref, dst_ref=ref,
            send_sem=xs_sem.at[way, block], recv_sem=xr_sem.at[way, block],
            device_id=(right if way % 2 == 0 else left, az), device_id_type=MESH,
        )

    def h_copy(part):
        return pltpu.make_async_remote_copy(
            src_ref=hsend.at[part], dst_ref=halo.at[pl.ds(64 * part, 64), :],
            send_sem=hs_sem.at[part], recv_sem=hr_sem.at[part],
            device_id=(acq, az + 1 if part == 0 else az - 1), device_id_type=MESH,
        )

    def have(block):
        x_copy(block, 0).start()
        x_copy(block, 1).start()

    def relay(block):
        x_copy(block, 0).wait_recv()
        x_copy(block, 2).start()
        x_copy(block, 1).wait_recv()
        x_copy(block, 3).start()

    def last(block):
        x_copy(block, 2).wait_recv()
        x_copy(block, 3).wait_recv()

    for part in range(2):
        edge_copy(part).wait()
        for g in range(4):
            picks = []
            for i in range(4):
                sc = 4 * g + i
                tile = edge[part, sc // 2, sc % 2].astype(F32)
                picks.append(tile[12:16] if part == 0 else tile[0:4])
            hsend[part, 16 * g : 16 * g + 16, :] = jnp.concatenate(picks, axis=0).astype(BF16)

    many = 2 + jnp.where(az < 15, 1, 0) + jnp.where(az > 0, 1, 0)
    many = many + jnp.where(zc < 3, 1, 0) + jnp.where(zc > 0, 1, 0)
    pl.semaphore_wait(barrier, many)
    for part in range(2):

        @pl.when((az < 15) & (az != 7) if part == 0 else (az > 0) & (az != 8))
        def _():
            h_copy(part).start()

        @pl.when(az == 0 if part == 0 else az == 15)
        def _():
            halo[64 * part : 64 * part + 64, :] = jnp.zeros((64, 2048), BF16)

    pl.when(zc < 3)(lambda: z_copy(zc, 1).start())
    pl.when(zc > 0)(lambda: z_copy(zc, 0).start())
    have(zc)

    build_weights(i0, i1, i2, i3, i4, azw, rgw, flag, eazw, ergw)

    def z_step(d):
        @pl.when(zc + d <= 3)
        def _():
            z_copy(zc + d, 0).wait_recv()
            pl.when(zc > 0)(lambda: z_copy(zc + d, 0).start())
            have(zc + d)

        @pl.when(zc - d >= 0)
        def _():
            z_copy(zc - d, 1).wait_recv()
            pl.when(zc < 3)(lambda: z_copy(zc - d, 1).start())
            have(zc - d)

    def pass_on(d):
        pl.when(zc + d <= 3)(lambda: relay(zc + d))
        pl.when(zc - d >= 0)(lambda: relay(zc - d))

    def pair(first, second):
        first()
        second()

    def far():
        pl.when(az == 7)(lambda: h_copy(0).start())
        pl.when(az == 8)(lambda: h_copy(1).start())

    def step_0():
        z_step(1)
        relay(zc)

    az_steps = [(2, step_0), (4, far)]
    rg_steps = [(10, lambda: z_step(2)), (20, lambda: pass_on(1)), (42, lambda: z_step(3)), (54, lambda: pass_on(2)), (64, lambda: None)]

    azimuth_own(xs, xt_a, xt_b, y, azw, lambda s: x_load(s).wait(), az_steps)
    range_filter(y, z, sums, rgw, flag, edge, et, rg_steps)
    edge_matrices(eazw, ewm, gmat)

    def edges(block):
        @pl.loop(0, 2)
        def _(h):
            for q in range(2):
                edge_cross(block * 4 + 2 * h + q, mt, gmat, ze, esum, flag)

    for g in range(4):
        block = order[g]
        if g == 2:
            pass_on(3)
        if g == 3:
            pl.when(az > 0)(lambda: h_copy(0).wait_recv())
            pl.when(az < 15)(lambda: h_copy(1).wait_recv())
            edge_filter(halo, et, ewm, ye, ze, ergw)
            for e in range(3):
                edges(order[e])
        last(block)

        @pl.loop(0, 2)
        def _(x):
            cross_slab(block * 4 + 2 * x, mt, m32, mp, z, sums, flag)

    edges(order[3])
    finish(sums, esum, out_ref)

    pl.when(az < 15)(lambda: h_copy(0).wait_send())
    pl.when(az > 0)(lambda: h_copy(1).wait_send())
    for block in range(4):
        pl.when((zc < 3) & (block <= zc))(lambda: z_copy(block, 1).wait_send())
        pl.when((zc > 0) & (block >= zc))(lambda: z_copy(block, 0).wait_send())
        for way in range(4):
            x_copy(block, way).wait_send()


def on_device(images, masters, az_shift, rg_shift, az_index, rg_index, segment):
    vmem = pl.BlockSpec(memory_space=pltpu.VMEM)
    dma = pltpu.SemaphoreType.DMA
    return pl.pallas_call(
        kernel,
        out_shape=jax.ShapeDtypeStruct((8, 2, 32, 128), F32),
        in_specs=[pl.BlockSpec(memory_space=pl.ANY)] + [vmem] * 6,
        out_specs=vmem,
        scratch_shapes=[
            pltpu.VMEM((2, 64, 2048), BF16),
            pltpu.VMEM((128, 2048), BF16),
            pltpu.VMEM((16, 4, 128, 128), BF16),
            pltpu.VMEM((8, 2, 128, 2048), BF16),
            pltpu.VMEM((2, 8, 2, 16, 2048), BF16),
            pltpu.VMEM((2, 2048, 128), BF16),
            pltpu.VMEM((2, 2048, 128), BF16),
            pltpu.VMEM((2, 2064 * 8, 128), F32),
            pltpu.VMEM((2, 2048, 8, 128), F32),
            pltpu.VMEM((5, 2048, 128), BF16),
            pltpu.VMEM((2064, 128), F32),
            pltpu.VMEM((2048, 128), F32),
            pltpu.VMEM((4, 256, 128), F32),
            pltpu.VMEM((2, 16, 128), F32),
            pltpu.VMEM((4, 128, 8, 128), F32),
            pltpu.VMEM((4, 128, 128), F32),
            pltpu.VMEM((9, 8, 128), F32),
            pltpu.VMEM((8, 8, 128), F32),
            pltpu.VMEM((3, 8, 128), F32),
            pltpu.VMEM((9, 8, 128), F32),
            pltpu.VMEM((9, 8, 128), F32),
            pltpu.VMEM((640, 256), BF16),
            pltpu.VMEM((256, 256), BF16),
            dma((8,)),
            dma((2,)),
            dma((2,)),
            dma((2,)),
            dma((2, 4)),
            dma((4,)),
            dma((4, 4)),
            dma((4, 4)),
        ],
        compiler_params=pltpu.CompilerParams(
            collective_id=0, has_side_effects=True, vmem_limit_bytes=60 * 2**20
        ),
        name="resample",
    )(images, masters, az_shift, rg_shift, az_index, rg_index, segment)


def solution(mesh):
    return jax.shard_map(
        on_device,
        mesh=mesh,
        in_specs=(
            P("acq", None, "az", None),
            P(None, None, "az", "acq"),
            P("acq", "az"),
            P("acq", "az"),
            P("acq", "az"),
            P("acq", "az"),
            P("acq", "az"),
        ),
        out_specs=P("acq", None, "az", None),
        check_vma=False,
    )
```

time: 49.5 us -> 44.3 us (0.89); the launches traced: 48.7 us -> 44.2 us
  Pallas kernels: 47 us -> 42.5 us
    pallas_call x1, Pallas kernels: 47 us -> 42.5 us  [on_device(): pl.pallas_call(kernel, out_shape=jax.ShapeDtypeStruct((8, 2, 32, 128), F3...]
where the time goes in v3:
time: 44.3 us; the launch traced here: 44.2 us
  Pallas kernels  42.5 us (96%)
  local copies, waits for them, and re-layouts  1.67 us (4%)
    pallas_call x1, Pallas kernels, on_device(): pl.pallas_call(kernel, out_shape=jax.ShapeDtypeStruct((8, 2, 32, 128), F3...  42.5 us
    unnamed x1, local copies, waits for them, and re-layouts  1.67 us

profile of v3, /device:TPU:25, one launch (start us, length us, event | category | flops | bytes accessed | tf_op | source)
XLA Modules:
  0.0 44.2 jit_solution(16694299412002421123)
XLA Ops:
  0.0 42.5 %resample.1 = f32[8,2,32,128]{3,2,1,0:T(8,128)} custom-call(bf16[8,2,128,2048]{3,2,1,0:T(8,128)(2,1)} %x_hbm.1, bf16[2,2,128,128]{3,2,1,0:T(8,128)(2,1)} %m_ref.1, s32[8,8]{1,0:T(8,128)} %i0.1, s32[8,8]{1,0:T(8,128)} %i1.1, s32[8,8]{1,0:T(8,128)} %i2.1, s32[8,8]{1,0:T(8,128)} %i3.1, s32[8,8]{1,0:T(8,128)} %i4.1), custom_call_target="tpu_custom_call" | custom-call | tf_op jit(solution)/shard_map/resample/pallas_call | solution.py:491
  42.5 1.7 %copy.9 = f32[8,2,32,128]{3,2,1,0:T(8,128)} copy(f32[8,2,32,128]{3,2,1,0:T(8,128)} %resample.1) | data formatting | bytes 524288

commit v4 on v3

--- a/solution.py
+++ b/solution.py
@@ -396,6 +396,9 @@
                 picks.append(tile[12:16] if part == 0 else tile[0:4])
             hsend[part, 16 * g : 16 * g + 16, :] = jnp.concatenate(picks, axis=0).astype(BF16)
 
+    build_weights(i0, i1, i2, i3, i4, azw, rgw, flag, eazw, ergw)
+    edge_matrices(eazw, ewm, gmat)
+
     many = 2 + jnp.where(az < 15, 1, 0) + jnp.where(az > 0, 1, 0)
     many = many + jnp.where(zc < 3, 1, 0) + jnp.where(zc > 0, 1, 0)
     pl.semaphore_wait(barrier, many)
@@ -412,8 +415,6 @@
     pl.when(zc < 3)(lambda: z_copy(zc, 1).start())
     pl.when(zc > 0)(lambda: z_copy(zc, 0).start())
     have(zc)
-
-    build_weights(i0, i1, i2, i3, i4, azw, rgw, flag, eazw, ergw)
 
     def z_step(d):
         @pl.when(zc + d <= 3)
@@ -449,7 +450,6 @@
 
     azimuth_own(xs, xt_a, xt_b, y, azw, lambda s: x_load(s).wait(), az_steps)
     range_filter(y, z, sums, rgw, flag, edge, et, rg_steps)
-    edge_matrices(eazw, ewm, gmat)
 
     def edges(block):
         @pl.loop(0, 2)

time: 44.3 us -> 44.4 us (level)
  no operation moved by 1% of the time
where the time goes in v4:
time: 44.4 us; the launch traced here: 44.3 us
  Pallas kernels  42.6 us (96%)
  local copies, waits for them, and re-layouts  1.67 us (4%)
    pallas_call x1, Pallas kernels, on_device(): pl.pallas_call(kernel, out_shape=jax.ShapeDtypeStruct((8, 2, 32, 128), F3...  42.6 us
    unnamed x1, local copies, waits for them, and re-layouts  1.67 us

profile of v4, /device:TPU:25, one launch (start us, length us, event | category | flops | bytes accessed | tf_op | source)
XLA Modules:
  0.0 44.3 jit_solution(9786203033814353851)
XLA Ops:
  0.0 42.6 %resample.1 = f32[8,2,32,128]{3,2,1,0:T(8,128)} custom-call(bf16[8,2,128,2048]{3,2,1,0:T(8,128)(2,1)} %x_hbm.1, bf16[2,2,128,128]{3,2,1,0:T(8,128)(2,1)} %m_ref.1, s32[8,8]{1,0:T(8,128)} %i0.1, s32[8,8]{1,0:T(8,128)} %i1.1, s32[8,8]{1,0:T(8,128)} %i2.1, s32[8,8]{1,0:T(8,128)} %i3.1, s32[8,8]{1,0:T(8,128)} %i4.1), custom_call_target="tpu_custom_call" | custom-call | tf_op jit(solution)/shard_map/resample/pallas_call | solution.py:491
  42.7 1.7 %copy.9 = f32[8,2,32,128]{3,2,1,0:T(8,128)} copy(f32[8,2,32,128]{3,2,1,0:T(8,128)} %resample.1) | data formatting | bytes 524288
